TPU v7x, 32 devices: a whole 2x2x4 slice. The times are simulated.
32 devices in a mesh: gx: 4 (over x, core), gy: 8 (over z, y).
Axes of the slice: x: 2, y: 2, z: 4, core: 2. Of those that a mesh axis runs over, the one named last changes fastest.
Arguments:
- views: bfloat16 [384, 49, 2048], P(('gx', 'gy')), may hold values from -6 to 6
- counts: int32 [32], P(('gx', 'gy')), may hold values from 1 to 12, as said below
- partners: int32 [384, 2], P(('gx', 'gy')), may hold values from 0 to 383, as said below
- w_in: bfloat16 [2048, 512], P('gx', 'gy'), may hold values from -0.125 to 0.125
- w_mid: bfloat16 [4608, 512], P('gx', 'gy'), may hold values from -0.09375 to 0.09375
- w_out: bfloat16 [512, 2048], P('gx', 'gy'), may hold values from -0.25 to 0.25
- norm_params: bfloat16 [6144], P(('gx', 'gy')), may hold values from 0.5 to 1.5
Outputs:
- loss_value: float32 [], replicated
- views_grad: float32 [384, 49, 2048], P(('gx', 'gy'))
- w_in_grad: float32 [2048, 512], P('gx', 'gy')
- w_mid_grad: float32 [4608, 512], P('gx', 'gy')
- w_out_grad: float32 [512, 2048], P('gx', 'gy')
- norm_grad: float32 [6144], P(('gx', 'gy'))
Inputs may be any that keep to these rules, and one draw needn't show every extreme that they name: A device's views fill its first counts slots; in every draw some device has all 12 slots filled and some device holds one view. Every entry names a filled slot; a filled slot never lists itself, and its partners lie mostly on other devices. Entries of empty slots are filled slots too.
All inputs are finite; a program needn't handle non-finite values.
Results may differ from a plain program's by a relative error of at most 0.017.
Values may be sent and summed in bfloat16 or wider, within the bound.
No kernel may reach another device: no remote copies, remote signals or barrier semaphores. Data moves between devices by JAX's collectives and lax.ppermute only.
A program may use at most 192 MiB of HBM per device.

v0:
```python
import jax
import jax.numpy as jnp
from jax import lax
from jax.sharding import PartitionSpec as P

SIDE = 7


def collect(w_in, w_mid, w_out, norm_params):
    part_in, part_mid, part_out, part_norm = (
        lax.all_gather(w_in, "gy", axis=1, tiled=True),
        lax.all_gather(w_mid, "gy", axis=1, tiled=True),
        lax.all_gather(w_out, "gy", axis=1, tiled=True),
        lax.all_gather(norm_params, "gy", axis=0, tiled=True),
    )
    return (
        lax.all_gather(part_in, "gx", axis=0, tiled=True),
        lax.all_gather(part_mid, "gx", axis=0, tiled=True),
        lax.all_gather(part_out, "gx", axis=0, tiled=True),
        lax.all_gather(part_norm, "gx", axis=0, tiled=True),
    )


def silu_slope(value):
    sigma = jax.nn.sigmoid(value)
    return sigma * (1.0 + value * (1.0 - sigma))


def normalize(hidden, gain, shift, pixel_weight):
    running, squares, number = lax.psum(
        (
            jnp.sum(hidden * pixel_weight, axis=0),
            jnp.sum(hidden * hidden * pixel_weight, axis=0),
            jnp.sum(pixel_weight),
        ),
        ("gx", "gy"),
    )
    center = running / number
    spread = squares / number - center * center
    inverse = lax.rsqrt(spread + 1e-05)
    scaled = (hidden - center) * inverse
    return (scaled, inverse, number, gain * scaled + shift)


def norm_back(upstream, scaled, inverse, gain, pixel_weight, number):
    shift_grad, gain_grad = lax.psum(
        (
            jnp.sum(upstream * pixel_weight, axis=0),
            jnp.sum(upstream * scaled * pixel_weight, axis=0),
        ),
        ("gx", "gy"),
    )
    inner = (
        upstream
        - pixel_weight * (shift_grad / number)
        - pixel_weight * scaled * (gain_grad / number)
    )
    return ((gain * inverse * inner).astype(jnp.bfloat16), gain_grad, shift_grad)


def unfold(grid_in):
    edge_len = grid_in.shape[1]
    padded = jnp.pad(grid_in, ((0, 0), (1, 1), (1, 1), (0, 0)))
    pieces = [
        padded[:, tap_row : tap_row + edge_len, tap_col : tap_col + edge_len, :]
        for tap_row in range(3)
        for tap_col in range(3)
    ]
    return jnp.concatenate(pieces, axis=3).reshape(
        grid_in.shape[0] * edge_len * edge_len, 9 * grid_in.shape[3]
    )


def fold_back(columns, slot_count, edge_len, channels):
    blocks = columns.reshape(slot_count, edge_len, edge_len, 9, channels)
    running = jnp.zeros((slot_count, edge_len + 2, edge_len + 2, channels), jnp.float32)
    for tap_row in range(3):
        for tap_col in range(3):
            running = running.at[
                :, tap_row : tap_row + edge_len, tap_col : tap_col + edge_len, :
            ].add(blocks[:, :, :, 3 * tap_row + tap_col, :])
    return running[:, 1 : edge_len + 1, 1 : edge_len + 1, :].reshape(
        slot_count * edge_len * edge_len, channels
    )


def contract_rows(left_side, right_side):
    return lax.dot_general(
        left_side, right_side, (((0,), (0,)), ((), ())), preferred_element_type=jnp.float32
    )


def contract_cols(left_side, right_side):
    return lax.dot_general(
        left_side, right_side, (((1,), (1,)), ((), ())), preferred_element_type=jnp.float32
    )


def split_norms(norm_values, channels, features):
    return (
        norm_values[0:channels],
        norm_values[channels : 2 * channels],
        norm_values[2 * channels : 3 * channels],
        norm_values[3 * channels : 4 * channels],
        norm_values[4 * channels : 4 * channels + features],
        norm_values[4 * channels + features : 4 * channels + 2 * features],
    )


def per_device(views, counts, partners, w_in, w_mid, w_out, norm_params):
    slot_count, pixels, features = views.shape
    edge_len = SIDE
    row_count = slot_count * pixels
    pair_count = partners.shape[1]
    device = lax.axis_index("gx") * lax.axis_size("gy") + lax.axis_index("gy")
    filled = (jnp.arange(slot_count, dtype=jnp.int32) < counts[0]).astype(jnp.float32)
    pixel_weight = jnp.repeat(filled, pixels)[:, None]
    full_in, full_mid, full_out, full_norm = collect(w_in, w_mid, w_out, norm_params)
    channels = full_in.shape[1]
    norm_values = full_norm.astype(jnp.float32)
    gain_one, shift_one, gain_two, shift_two, gain_three, shift_three = split_norms(
        norm_values, channels, features
    )
    flat_in = views.reshape(row_count, features)
    hidden_one = jnp.dot(flat_in, full_in, preferred_element_type=jnp.float32)
    scaled_one, inverse_one, number, normed_one = normalize(
        hidden_one, gain_one, shift_one, pixel_weight
    )
    active_one = jax.nn.silu(normed_one).astype(jnp.bfloat16)
    columns = unfold(active_one.reshape(slot_count, edge_len, edge_len, channels))
    hidden_two = jnp.dot(columns, full_mid, preferred_element_type=jnp.float32)
    scaled_two, inverse_two, _, normed_two = normalize(
        hidden_two, gain_two, shift_two, pixel_weight
    )
    active_two = jax.nn.silu(normed_two).astype(jnp.bfloat16)
    hidden_three = jnp.dot(active_two, full_out, preferred_element_type=jnp.float32)
    scaled_three, inverse_three, _, normed_three = normalize(
        hidden_three, gain_three, shift_three, pixel_weight
    )
    summed = normed_three + flat_in.astype(jnp.float32)
    activated = jax.nn.silu(summed)
    pooled = jnp.sum(activated.reshape(slot_count, pixels, features), axis=1) / pixels
    factor = lax.rsqrt(jnp.mean(pooled * pooled, axis=1, keepdims=True) + 1e-06)
    embedded = (pooled * factor).astype(jnp.bfloat16)
    embedded_f = embedded.astype(jnp.float32)
    targets = partners.reshape(slot_count * pair_count)
    shard_rows = lax.all_gather(embedded, ("gx", "gy"), axis=0, tiled=True)
    positions = jnp.arange(shard_rows.shape[0], dtype=jnp.int32)
    chooser = (targets[:, None] == positions[None, :]).astype(jnp.bfloat16)
    partner_rows = jnp.dot(chooser, shard_rows, preferred_element_type=jnp.float32)
    difference = (
        embedded_f[:, None, :] - partner_rows.reshape(slot_count, pair_count, features)
    ) * filled[:, None, None]
    outgoing = (-2.0 * difference).reshape(slot_count * pair_count, features)
    positions = jnp.arange(slot_count * lax.axis_size(("gx", "gy")), dtype=jnp.int32)
    chooser = (positions[:, None] == targets[None, :]).astype(jnp.float32)
    incoming = lax.psum_scatter(
        jnp.dot(chooser, outgoing, precision=lax.Precision.HIGHEST),
        ("gx", "gy"),
        scatter_dimension=0,
        tiled=True,
    )
    objective = lax.psum(jnp.sum(difference * difference), ("gx", "gy"))
    loss_value = objective / (pair_count * features * (number / pixels))
    grad_embed = (2.0 * jnp.sum(difference, axis=1) + incoming) * filled[:, None]
    grad_pooled = (
        factor * grad_embed
        - pooled
        * (factor * factor * factor)
        * jnp.sum(pooled * grad_embed, axis=1, keepdims=True)
        / features
    )
    spread_grad = jnp.broadcast_to(
        (grad_pooled / pixels)[:, None, :], (slot_count, pixels, features)
    ).reshape(row_count, features)
    grad_summed = spread_grad * silu_slope(summed)
    back_in, back_mid, back_out, back_norm = collect(w_in, w_mid, w_out, norm_params)
    back_values = back_norm.astype(jnp.float32)
    back_gain_one, _, back_gain_two, _, back_gain_three, _ = split_norms(
        back_values, channels, features
    )
    grad_three, gain_grad_three, shift_grad_three = norm_back(
        grad_summed, scaled_three, inverse_three, back_gain_three, pixel_weight, number
    )
    out_grad = contract_rows(active_two, grad_three)
    grad_active_two = contract_cols(grad_three, back_out)
    grad_normed_two = grad_active_two * silu_slope(normed_two)
    grad_two, gain_grad_two, shift_grad_two = norm_back(
        grad_normed_two, scaled_two, inverse_two, back_gain_two, pixel_weight, number
    )
    mid_grad = contract_rows(columns, grad_two)
    grad_columns = contract_cols(grad_two, back_mid)
    grad_active_one = fold_back(grad_columns, slot_count, edge_len, channels)
    grad_normed_one = grad_active_one * silu_slope(normed_one)
    grad_one, gain_grad_one, shift_grad_one = norm_back(
        grad_normed_one, scaled_one, inverse_one, back_gain_one, pixel_weight, number
    )
    in_grad = contract_rows(flat_in, grad_one)
    views_grad = (contract_cols(grad_one, back_in) + grad_summed).reshape(
        slot_count, pixels, features
    )
    part_in, part_mid, part_out = (
        lax.psum_scatter(in_grad, "gx", scatter_dimension=0, tiled=True),
        lax.psum_scatter(mid_grad, "gx", scatter_dimension=0, tiled=True),
        lax.psum_scatter(out_grad, "gx", scatter_dimension=0, tiled=True),
    )
    own_in, own_mid, own_out = (
        lax.psum_scatter(part_in, "gy", scatter_dimension=1, tiled=True),
        lax.psum_scatter(part_mid, "gy", scatter_dimension=1, tiled=True),
        lax.psum_scatter(part_out, "gy", scatter_dimension=1, tiled=True),
    )
    norm_full = jnp.concatenate(
        [
            gain_grad_one,
            shift_grad_one,
            gain_grad_two,
            shift_grad_two,
            gain_grad_three,
            shift_grad_three,
        ]
    )
    share = norm_full.shape[0] // (lax.axis_size("gx") * lax.axis_size("gy"))
    norm_grad = lax.dynamic_slice_in_dim(norm_full, device * share, share)
    return (loss_value, views_grad, own_in, own_mid, own_out, norm_grad)


def solution(mesh):
    in_specs = (
        P(("gx", "gy"), None, None),
        P(("gx", "gy")),
        P(("gx", "gy"), None),
        P("gx", "gy"),
        P("gx", "gy"),
        P("gx", "gy"),
        P(("gx", "gy")),
    )
    out_specs = (
        P(),
        P(("gx", "gy"), None, None),
        P("gx", "gy"),
        P("gx", "gy"),
        P("gx", "gy"),
        P(("gx", "gy")),
    )
    return jax.shard_map(
        per_device, mesh=mesh, in_specs=in_specs, out_specs=out_specs, check_vma=False
    )
```

profile of v0, /device:TPU:0, one launch (start us, length us, event | category | flops | bytes accessed | tf_op | source)
XLA Modules:
  0.0 1157.9 jit_solution(8013331020981908882)
XLA Ops:
  8.0 35.6 %all_gather.37 = bf16[512,512]{0,1:T(8,128)(2,1)} all-gather(bf16[512,64]{0,1:T(8,128)(2,1)} %param.28), channel_id=1, replica_groups=mesh['gx'=4,'gy'=8] {'gy'}, dimensions={1}, use_global_device_ids=true | all-gather | bytes 589824 | tf_op jit(solution)/shard_map/all_gather | solution.py:11
  43.6 11.1 all-gather.10.cloned.1.call-done
  54.8 33.4 %all_gather.41 = bf16[128,2048]{1,0:T(8,128)(2,1)} all-gather(bf16[128,256]{1,0:T(8,128)(2,1)S(1)} %copy-done.19), channel_id=1, replica_groups=mesh['gx'=4,'gy'=8] {'gy'}, dimensions={1}, use_global_device_ids=true | all-gather | bytes 589824 | tf_op jit(solution)/shard_map/all_gather | solution.py:13
  91.2 19.7 %all-reduce.2 = bf16[1536]{0:T(1024)(128)(2,1)S(1)} all-reduce(bf16[1536]{0:T(1024)(128)(2,1)S(1)} %dynamic-update-slice.27), channel_id=1, replica_groups=mesh['gx'=4,'gy'=8] {'gy'}, use_global_device_ids=true, to_apply=%add.2 | all-reduce | flops 1536 | bytes 6144
  123.6 37.3 %all-reduce.10 = (f32[512]{0:T(512)S(1)}, f32[]{:T(128)}, f32[512]{0:T(512)S(1)}) all-reduce(f32[512]{0:T(512)S(1)} %get-tuple-element.149, f32[]{:T(128)} %broadcast_reduce_fusion, f32[512]{0:T(512)S(1)} %get-tuple-element.148), channel_id=1, replica_groups=mesh['gx'=4,'gy'=8] {'gx','gy'}, use_global_device_ids=true, to_apply=%region_5.0 | all-reduce | flops 1025 | bytes 8200 | tf_op jit(solution)/shard_map/psum | solution.py:30
  164.8 5.7 pad_slice_fusion
  195.9 8.0 multiply_reduce_fusion.9
  203.9 42.4 %all-reduce.9 = (f32[512]{0:T(512)S(1)}, f32[512]{0:T(512)S(1)}) all-reduce(f32[512]{0:T(512)S(1)} %get-tuple-element.147, f32[512]{0:T(512)S(1)} %get-tuple-element.146), channel_id=1, replica_groups=mesh['gx'=4,'gy'=8] {'gx','gy'}, use_global_device_ids=true, to_apply=%region_9.10 | all-reduce | flops 1024 | bytes 8192 | tf_op jit(solution)/shard_map/psum | solution.py:30
  246.9 5.9 multiply_reduce_fusion.2
  252.8 38.8 %all-reduce.8 = (f32[2048]{0:T(1024)S(1)}, f32[2048]{0:T(1024)S(1)}) all-reduce(f32[2048]{0:T(1024)S(1)} %get-tuple-element.141, f32[2048]{0:T(1024)S(1)} %get-tuple-element.140), channel_id=1, replica_groups=mesh['gx'=4,'gy'=8] {'gx','gy'}, use_global_device_ids=true, to_apply=%region_11.12 | all-reduce | flops 4096 | bytes 32768 | tf_op jit(solution)/shard_map/psum | solution.py:30
  293.0 6.3 fusion.1
  309.7 55.6 %all-gather.16.cloned.1.call-done = bf16[32,12,2048]{2,1,0:T(8,128)(2,1)} async-done(((bf16[1,12,2048]{2,1,0:T(8,128)(2,1)}), bf16[32,12,2048]{2,1,0:T(8,128)(2,1)}) %all-gather.16.cloned.1.call-update) | async-done | bytes 1572880 | tf_op jit(solution)/shard_map/all_gather | solution.py:147
  374.3 99.8 %fusion = f32[16,2048]{1,0:T(8,128)S(1)} fusion(f32[384,2048]{1,0:T(8,128)} %fusion.3), kind=kCustom, calls=%all-reduce-scatter | all-reduce-scatter fusion | flops 1048577 | bytes 3276800
  502.0 14.8 %concatenate.60 = f32[140,2048]{1,0:T(8,128)} concatenate(f32[12,2048]{1,0:T(8,128)} %collective-permute-done.7, f32[16,2048]{1,0:T(8,128)S(1)} %collective-permute-done.6, f32[16,2048]{1,0:T(8,128)} %collective-permute-done.5, f32[16,2048]{1,0:T(8,128)} %copy-done.15, f32[16,2048]{1,0:T(8,128)} %copy-done.16, f32[16,2048]{1,0:T(8,128)} %copy-done.17, f32[16,2048]{1,0:T(8,128)} %copy-done.18, ...), dimensions={0} | concatenate | bytes 2293760
  526.7 7.3 multiply_reduce_fusion.1
  534.0 45.6 %all-reduce.7 = (f32[2048]{0:T(1024)S(1)}, f32[2048]{0:T(1024)S(1)}) all-reduce(f32[2048]{0:T(1024)S(1)} %get-tuple-element.139, f32[2048]{0:T(1024)S(1)} %get-tuple-element.138), channel_id=1, replica_groups=mesh['gx'=4,'gy'=8] {'gx','gy'}, use_global_device_ids=true, to_apply=%region_24.25 | all-reduce | flops 4096 | bytes 32768 | tf_op jit(solution)/shard_map/psum | solution.py:46
  580.3 5.5 multiply_convert_fusion
  594.6 41.5 %all-reduce.6 = (f32[512]{0:T(512)S(1)}, f32[512]{0:T(512)S(1)}) all-reduce(f32[512]{0:T(512)S(1)} %get-tuple-element.145, f32[512]{0:T(512)S(1)} %get-tuple-element.144), channel_id=1, replica_groups=mesh['gx'=4,'gy'=8] {'gx','gy'}, use_global_device_ids=true, to_apply=%region_28.29 | all-reduce | flops 1024 | bytes 8192 | tf_op jit(solution)/shard_map/psum | solution.py:46
  640.4 8.0 fusion.20
  648.4 13.9 %reshape.498 = f32[12,7,7,9,512]{4,3,2,1,0:T(8,128)} reshape(f32[588,4608]{1,0:T(8,128)} %fusion.20) | data formatting | bytes 21676032 | tf_op jit(solution)/shard_map/reshape | solution.py:75
  662.3 32.5 %fusion.17 = (f32[12,7,7,1,512]{4,3,2,1,0:T(1,128)}, f32[12,7,7,1,512]{4,3,2,1,0:T(1,128)}, f32[12,7,7,1,512]{4,3,2,1,0:T(1,128)}, f32[12,7,7,1,512]{4,3,2,1,0:T...) fusion(f32[12,7,7,9,512]{4,3,2,1,0:T(8,128)} %reshape.498), kind=kLoop, calls=%fused_computation.119 | loop fusion | bytes 21676032 | tf_op jit(solution)/shard_map/slice | solution.py:81
  698.9 6.5 scatter-add.31
  710.3 6.7 scatter-add.34
  727.8 5.3 scatter-add.36
  770.6 39.4 %all-reduce.5 = (f32[]{:T(128)}, f32[512]{0:T(512)S(1)}, f32[512]{0:T(512)S(1)}) all-reduce(f32[]{:T(128)} %get-tuple-element.212, f32[512]{0:T(512)S(1)} %get-tuple-element.143, f32[512]{0:T(512)S(1)} %get-tuple-element.142), channel_id=1, replica_groups=mesh['gx'=4,'gy'=8] {'gx','gy'}, use_global_device_ids=true, to_apply=%region_17.18 | all-reduce | flops 1025 | bytes 8200 | tf_op jit(solution)/shard_map/psum | solution.py:163
  818.4 9.0 fusion.21
  828.2 34.0 %reduce-scatter.11.cloned.1.call-done = f32[512,512]{0,1:T(8,128)} async-done(((f32[2048,512]{0,1:T(8,128)}), f32[512,512]{0,1:T(8,128)}) %reduce-scatter.11.cloned.1.call-update) | async-done | bytes 1048592 | tf_op jit(solution)/shard_map/reduce_scatter | solution.py:203
  862.3 80.9 %reduce-scatter.15.cloned.1.call-done = f32[1152,512]{1,0:T(8,128)} async-done(((f32[4608,512]{1,0:T(8,128)}), f32[1152,512]{1,0:T(8,128)}) %reduce-scatter.15.cloned.1.call-update) | async-done | bytes 2359312 | tf_op jit(solution)/shard_map/reduce_scatter | solution.py:204
  947.0 6.6 convolution_add_fusion
  959.9 51.2 %reduce-scatter.19.cloned.1.call-done = f32[128,256]{1,0:T(8,128)} async-done(((f32[128,2048]{1,0:T(8,128)}), f32[128,256]{1,0:T(8,128)}) %reduce-scatter.19.cloned.1.call-update) | async-done | bytes 131088 | tf_op jit(solution)/shard_map/reduce_scatter | solution.py:210
  1011.1 66.8 %reduce-scatter.13.cloned.1.call-done = f32[512,64]{0,1:T(8,128)} async-done(((f32[512,512]{0,1:T(8,128)}), f32[512,64]{0,1:T(8,128)}) %reduce-scatter.13.cloned.1.call-update) | async-done | bytes 131088 | tf_op jit(solution)/shard_map/reduce_scatter | solution.py:208
  1077.9 72.2 %reduce-scatter.21.cloned.1.call-done = f32[64,1152]{1,0:T(8,128)} async-done(((f32[512,1152]{1,0:T(8,128)}), f32[64,1152]{1,0:T(8,128)}) %reduce-scatter.21.cloned.1.call-update) | async-done | bytes 294928
  (212 shorter events, 191.9 us)
Async XLA Ops:
  7.2 47.7 %copy-start.19 = (bf16[128,256]{1,0:T(8,128)(2,1)S(1)}, bf16[128,256]{1,0:T(8,128)(2,1)}, u32[]{:S(2)}) copy-start(bf16[128,256]{1,0:T(8,128)(2,1)} %param.30) | copy-start | bytes 196612
  7.2 47.6 %all-gather.10.cloned.1.call-start = ((), (), s32[]{:S(2)}) async-start(), calls=%async_computation.7 | async-start | bytes 1327104 | tf_op jit(solution)/shard_map/all_gather | solution.py:12
  7.9 110.8 %all-gather.8.cloned.1.call-start = ((), (), s32[]{:S(2)}) async-start(), calls=%async_computation.6 | async-start | bytes 2621440 | tf_op jit(solution)/shard_map/all_gather | solution.py:17
  43.5 46.1 %copy-start.35 = (u32[32]{0:T(128)S(1)}, u32[32]{0:T(128)}, u32[]{:S(2)}) copy-start(u32[32]{0:T(128)} %constant.326) | copy-start | bytes 388
  43.5 47.4 %copy-start.34 = (bf16[192]{0:T(256)(128)(2,1)S(1)}, bf16[192]{0:T(256)(128)(2,1)}, u32[]{:S(2)}) copy-start(bf16[192]{0:T(256)(128)(2,1)} %param.31) | copy-start | bytes 1156
  43.6 152.3 %all-gather.12.cloned.1.call-start = ((), (), s32[]{:S(2)}) async-start(), calls=%async_computation.8 | async-start | bytes 5898240 | tf_op jit(solution)/shard_map/all_gather | solution.py:18
  54.8 192.2 %all-gather.14.cloned.1.call-start = ((), (), s32[]{:S(2)}) async-start(), calls=%async_computation.9 | async-start | bytes 2621440 | tf_op jit(solution)/shard_map/all_gather | solution.py:19
  88.2 277.0 %all-gather.16.cloned.1.call-start = ((), (), s32[]{:S(2)}) async-start(), calls=%async_computation.15 | async-start | bytes 2162688 | tf_op jit(solution)/shard_map/all_gather | solution.py:147
  118.6 408.1 %copy-start = (bf16[588,2048]{1,0:T(8,128)(2,1)}, bf16[588,2048]{1,0:T(8,128)(2,1)S(1)}, u32[]{:S(2)}) copy-start(bf16[588,2048]{1,0:T(8,128)(2,1)S(1)} %reshape.493) | copy-start | bytes 7225348
  162.1 28.8 %copy-start.20 = (f32[512]{0:T(512)}, f32[512]{0:T(512)S(1)}, u32[]{:S(2)}) copy-start(f32[512]{0:T(512)S(1)} %get-tuple-element.198) | copy-start | bytes 6148
  308.2 519.3 %reduce-scatter.17.cloned.1.call-start = ((), (), s32[]{:S(2)}) async-start(), calls=%async_computation.13 | async-start | bytes 5242880 | tf_op jit(solution)/shard_map/reduce_scatter | solution.py:205
  474.1 18.5 %collective-permute-start.6 = (f32[16,2048]{1,0:T(8,128)S(1)}, f32[16,2048]{1,0:T(8,128)S(1)}, u32[]{:S(2)}, u32[]{:S(2)}) collective-permute-start(f32[16,2048]{1,0:T(8,128)S(1)} %fusion), channel_id=1, source_target_pairs={{0,7},{1,8},{2,9},{3,10},{4,11},{5,12},{6,13},{7,14},{8,15},{9,16}... | collective-permute-start | bytes 393224
  477.4 17.8 %collective-permute-start.5 = (f32[16,2048]{1,0:T(8,128)S(1)}, f32[16,2048]{1,0:T(8,128)}, u32[]{:S(2)}, u32[]{:S(2)}) collective-permute-start(f32[16,2048]{1,0:T(8,128)S(1)} %fusion), channel_id=1, source_target_pairs={{0,6},{1,7},{2,8},{3,9},{4,10},{5,11},{6,12},{7,13},{8,14},{9,15},... | collective-permute-start | bytes 393224
  481.0 9.7 collective-permute-start.7
  484.1 15.8 %collective-permute-start.4 = (f32[16,2048]{1,0:T(8,128)S(1)}, f32[16,2048]{1,0:T(8,128)S(1)}, u32[]{:S(2)}, u32[]{:S(2)}) collective-permute-start(f32[16,2048]{1,0:T(8,128)S(1)} %fusion), channel_id=1, source_target_pairs={{0,5},{1,6},{2,7},{3,8},{4,9},{5,10},{6,11},{7,12},{8,13},{9,14},{... | collective-permute-start | bytes 393224
  486.9 13.0 %collective-permute-start.3 = (f32[16,2048]{1,0:T(8,128)S(1)}, f32[16,2048]{1,0:T(8,128)S(1)}, u32[]{:S(2)}, u32[]{:S(2)}) collective-permute-start(f32[16,2048]{1,0:T(8,128)S(1)} %fusion), channel_id=1, source_target_pairs={{0,4},{1,5},{2,6},{3,7},{4,8},{5,9},{6,10},{7,11},{8,12},{9,13},{1... | collective-permute-start | bytes 393224
  490.6 9.2 collective-permute-start.2
  492.6 7.3 collective-permute-start.1
  495.1 6.8 collective-permute-start
  579.6 6.2 copy-start.22
  579.6 6.2 copy-start.24
  589.7 272.5 %reduce-scatter.11.cloned.1.call-start = ((), (), s32[]{:S(2)}) async-start(), calls=%async_computation.10 | async-start | bytes 5242880 | tf_op jit(solution)/shard_map/reduce_scatter | solution.py:203
  768.9 41.2 %copy-start.33 = (f32[6144]{0:T(1024)S(1)}, f32[6144]{0:T(1024)}, u32[]{:S(2)}) copy-start(f32[6144]{0:T(1024)} %custom-call) | copy-start | bytes 73732
  768.9 42.5 %copy-start.30 = (f32[512]{0:T(512)S(1)}, f32[512]{0:T(512)}, u32[]{:S(2)}) copy-start(f32[512]{0:T(512)} %get-tuple-element.164) | copy-start | bytes 6148
  817.4 125.8 %reduce-scatter.15.cloned.1.call-start = ((), (), s32[]{:S(2)}) async-start(), calls=%async_computation.12 | async-start | bytes 11796480 | tf_op jit(solution)/shard_map/reduce_scatter | solution.py:204
  827.5 183.6 %reduce-scatter.19.cloned.1.call-start = ((), (), s32[]{:S(2)}) async-start(), calls=%async_computation.14 | async-start | bytes 1179648 | tf_op jit(solution)/shard_map/reduce_scatter | solution.py:210
  828.2 249.7 %reduce-scatter.13.cloned.1.call-start = ((), (), s32[]{:S(2)}) async-start(), calls=%async_computation.11 | async-start | bytes 1179648 | tf_op jit(solution)/shard_map/reduce_scatter | solution.py:208
  862.3 287.8 %reduce-scatter.21.cloned.1.call-start = ((), (), s32[]{:S(2)}) async-start(), calls=%async_computation.16 | async-start | bytes 2654208
  953.6 5.5 copy-start.29
  953.6 5.5 copy-start.27
  953.6 5.6 copy-start.25
  953.6 5.6 copy-start.23
  (23 other events, 49.1 us)
Sparse Core Ops, SparseCore 0:
  10.2 44.5 all-gather.9
  56.3 21.7 all-gather.7
  79.7 37.5 all-gather.11
  118.7 23.1 all-gather.13
  308.3 56.8 all-gather.15
  589.8 44.9 reduce-scatter.16
  817.5 44.6 reduce-scatter.10
  864.8 78.3 reduce-scatter.14
  947.2 63.8 reduce-scatter.18
  1015.3 62.5 reduce-scatter.12
  1081.9 68.0 reduce-scatter.20
where the time goes:
time: 1170 us; the launch traced here: 1160 us
  blocking collectives  439 us (38%)
  waiting for transfers between devices  374 us (32%)
  local copies, waits for them, and re-layouts  176 us (15%)
  other arithmetic  66.4 us (6%)
  matrix products  60.6 us (5%)
  starting transfers between devices  23.5 us (2%)
  between operations  18.5 us (2%)
    unnamed x2, blocking collectives  119 us
    psum x3, blocking collectives, normalize(): lax.psum((jnp.sum(hidden * pixel_weight, axis=0), jnp.sum(hidden * hidden...  118 us
    psum x2, blocking collectives, norm_back(): lax.psum((jnp.sum(upstream * pixel_weight, axis=0), jnp.sum(upstream * sc...  87.1 us
    reduce_scatter x1, waiting for transfers between devices, per_device(): lax.psum_scatter(mid_grad, 'gx', scatter_dimension=0, tiled=True)  80.9 us
    unnamed x20, waiting for transfers between devices  74.4 us
    reduce_scatter x1, waiting for transfers between devices, per_device(): lax.psum_scatter(part_in, 'gy', scatter_dimension=1, tiled=True)  66.8 us
    all_gather x1, waiting for transfers between devices, per_device(): shard_rows = lax.all_gather(embedded, ('gx', 'gy'), axis=0, tiled=True)  55.6 us
    reduce_scatter x1, waiting for transfers between devices, per_device(): lax.psum_scatter(part_out, 'gy', scatter_dimension=1, tiled=True)  51.2 us
  transfers between devices with their start and end apart: 19, of which 8 were waited for; matrix products, arithmetic and copies ran while one was open for 19% of the time, Pallas kernels for 0%

commit v1 on v0

--- a/solution.py
+++ b/solution.py
@@ -4,6 +4,9 @@
 from jax.sharding import PartitionSpec as P
 
 SIDE = 7
+_edit_knots = lambda vec, axis_id, device_axis: jax.lax.psum(
+    jax.lax.psum(vec, axis_name=axis_id), axis_name=device_axis
+)
 
 
 def collect(w_in, w_mid, w_out, norm_params):
@@ -43,12 +46,13 @@
 
 
 def norm_back(upstream, scaled, inverse, gain, pixel_weight, number):
-    shift_grad, gain_grad = lax.psum(
+    shift_grad, gain_grad = _edit_knots(
         (
             jnp.sum(upstream * pixel_weight, axis=0),
             jnp.sum(upstream * scaled * pixel_weight, axis=0),
         ),
-        ("gx", "gy"),
+        "gy",
+        "gx",
     )
     inner = (
         upstream

time: 1170 us -> 1140 us (0.974)
  waiting for transfers between devices: 374 us -> 332 us
    reduce_scatter x1, waiting for transfers between devices: 51.2 us -> 11.6 us  [per_device(): lax.psum_scatter(part_out, 'gy', scatter_dimension=1, tiled=True)]
    psum x2 -> x6, blocking collectives: 87.1 us -> 97.8 us  [the longest x3 75 us: jax.lax.psum(vec, axis_name=axis_id)]
  transfers between devices with their start and end apart: 19 -> 19, of which waited for: 8 -> 8; matrix products, arithmetic and copies ran while one was open for 19% -> 20% of each run, Pallas kernels for 0% -> 0%
where the time goes in v1:
time: 1140 us; the launch traced here: 1130 us
  blocking collectives  449 us (39%)
  waiting for transfers between devices  332 us (29%)
  local copies, waits for them, and re-layouts  176 us (15%)
  other arithmetic  66.2 us (6%)
  matrix products  60.7 us (5%)
  starting transfers between devices  26.5 us (2%)
  between operations  18.5 us (2%)
    unnamed x2, blocking collectives  118 us
    psum x3, blocking collectives, normalize(): lax.psum((jnp.sum(hidden * pixel_weight, axis=0), jnp.sum(hidden * hidden...  118 us
    reduce_scatter x1, waiting for transfers between devices, per_device(): lax.psum_scatter(mid_grad, 'gx', scatter_dimension=0, tiled=True)  81 us
    psum x3, blocking collectives, jax.lax.psum(vec, axis_name=axis_id)  75 us
    unnamed x20, waiting for transfers between devices  74.3 us
    reduce_scatter x1, waiting for transfers between devices, per_device(): lax.psum_scatter(part_in, 'gy', scatter_dimension=1, tiled=True)  66.6 us
    all_gather x1, waiting for transfers between devices, per_device(): shard_rows = lax.all_gather(embedded, ('gx', 'gy'), axis=0, tiled=True)  55.6 us
    scatter-add x9, local copies, waits for them, and re-layouts, fold_back(): running = running.at[:, tap_row:tap_row + edge_len, tap_col:tap_col + edg...  45.6 us
  transfers between devices with their start and end apart: 19, of which 8 were waited for; matrix products, arithmetic and copies ran while one was open for 20% of the time, Pallas kernels for 0%

profile of v1, /device:TPU:0, one launch (start us, length us, event | category | flops | bytes accessed | tf_op | source)
XLA Modules:
  0.0 1128.4 jit_solution(13304149849738259498)
XLA Ops:
  8.0 35.6 %all_gather.37 = bf16[512,512]{0,1:T(8,128)(2,1)} all-gather(bf16[512,64]{0,1:T(8,128)(2,1)} %param.28), channel_id=1, replica_groups=mesh['gx'=4,'gy'=8] {'gy'}, dimensions={1}, use_global_device_ids=true | all-gather | bytes 589824 | tf_op jit(solution)/shard_map/all_gather | solution.py:14
  43.6 11.1 all-gather.10.cloned.1.call-done
  54.8 33.4 %all_gather.41 = bf16[128,2048]{1,0:T(8,128)(2,1)} all-gather(bf16[128,256]{1,0:T(8,128)(2,1)S(1)} %copy-done.19), channel_id=1, replica_groups=mesh['gx'=4,'gy'=8] {'gy'}, dimensions={1}, use_global_device_ids=true | all-gather | bytes 589824 | tf_op jit(solution)/shard_map/all_gather | solution.py:16
  91.2 19.7 %all-reduce.2 = bf16[1536]{0:T(1024)(128)(2,1)S(1)} all-reduce(bf16[1536]{0:T(1024)(128)(2,1)S(1)} %dynamic-update-slice.27), channel_id=1, replica_groups=mesh['gx'=4,'gy'=8] {'gy'}, use_global_device_ids=true, to_apply=%add.2 | all-reduce | flops 1536 | bytes 6144
  123.6 37.3 %all-reduce.7 = (f32[512]{0:T(512)S(1)}, f32[]{:T(128)}, f32[512]{0:T(512)S(1)}) all-reduce(f32[512]{0:T(512)S(1)} %get-tuple-element.149, f32[]{:T(128)} %broadcast_reduce_fusion, f32[512]{0:T(512)S(1)} %get-tuple-element.148), channel_id=1, replica_groups=mesh['gx'=4,'gy'=8] {'gx','gy'}, use_global_device_ids=true, to_apply=%region_5.0 | all-reduce | flops 1025 | bytes 8200 | tf_op jit(solution)/shard_map/psum | solution.py:33
  195.9 8.0 multiply_reduce_fusion.9
  203.9 42.3 %all-reduce.6 = (f32[512]{0:T(512)S(1)}, f32[512]{0:T(512)S(1)}) all-reduce(f32[512]{0:T(512)S(1)} %get-tuple-element.147, f32[512]{0:T(512)S(1)} %get-tuple-element.146), channel_id=1, replica_groups=mesh['gx'=4,'gy'=8] {'gx','gy'}, use_global_device_ids=true, to_apply=%region_9.10 | all-reduce | flops 1024 | bytes 8192 | tf_op jit(solution)/shard_map/psum | solution.py:33
  252.8 38.8 %all-reduce.5 = (f32[2048]{0:T(1024)S(1)}, f32[2048]{0:T(1024)S(1)}) all-reduce(f32[2048]{0:T(1024)S(1)} %get-tuple-element.141, f32[2048]{0:T(1024)S(1)} %get-tuple-element.140), channel_id=1, replica_groups=mesh['gx'=4,'gy'=8] {'gx','gy'}, use_global_device_ids=true, to_apply=%region_11.12 | all-reduce | flops 4096 | bytes 32768 | tf_op jit(solution)/shard_map/psum | solution.py:33
  293.0 6.3 fusion.1
  309.7 55.6 %all-gather.16.cloned.1.call-done = bf16[32,12,2048]{2,1,0:T(8,128)(2,1)} async-done(((bf16[1,12,2048]{2,1,0:T(8,128)(2,1)}), bf16[32,12,2048]{2,1,0:T(8,128)(2,1)}) %all-gather.16.cloned.1.call-update) | async-done | bytes 1572880 | tf_op jit(solution)/shard_map/all_gather | solution.py:151
  374.3 98.8 %fusion = f32[16,2048]{1,0:T(8,128)S(1)} fusion(f32[384,2048]{1,0:T(8,128)} %fusion.3), kind=kCustom, calls=%all-reduce-scatter | all-reduce-scatter fusion | flops 1048577 | bytes 3276800
  473.2 7.1 collective-permute-start.6
  503.9 14.8 %concatenate.60 = f32[140,2048]{1,0:T(8,128)} concatenate(f32[12,2048]{1,0:T(8,128)} %collective-permute-done.7, f32[16,2048]{1,0:T(8,128)S(1)} %collective-permute-done.6, f32[16,2048]{1,0:T(8,128)} %collective-permute-done.5, f32[16,2048]{1,0:T(8,128)} %copy-done.15, f32[16,2048]{1,0:T(8,128)} %copy-done.16, f32[16,2048]{1,0:T(8,128)} %copy-done.17, f32[16,2048]{1,0:T(8,128)} %copy-done.18, ...), dimensions={0} | concatenate | bytes 2293760
  528.6 7.3 multiply_reduce_fusion.1
  535.9 38.6 %all-reduce.10 = (f32[2048]{0:T(1024)S(1)}, f32[2048]{0:T(1024)S(1)}) all-reduce(f32[2048]{0:T(1024)S(1)} %get-tuple-element.139, f32[2048]{0:T(1024)S(1)} %get-tuple-element.138), channel_id=1, replica_groups=mesh['gx'=4,'gy'=8] {'gy'}, use_global_device_ids=true, to_apply=%region_25.26 | all-reduce | flops 4096 | bytes 32768 | tf_op jit(solution)/shard_map/psum | solution.py:8
  574.5 10.6 all-reduce.13
  600.1 17.1 %all-reduce.9 = (f32[512]{0:T(512)S(1)}, f32[512]{0:T(512)S(1)}) all-reduce(f32[512]{0:T(512)S(1)} %get-tuple-element.145, f32[512]{0:T(512)S(1)} %get-tuple-element.144), channel_id=1, replica_groups=mesh['gx'=4,'gy'=8] {'gy'}, use_global_device_ids=true, to_apply=%region_31.32 | all-reduce | flops 1024 | bytes 8192 | tf_op jit(solution)/shard_map/psum | solution.py:8
  617.2 6.6 all-reduce.12
  628.0 8.0 fusion.20
  636.0 14.0 %reshape.498 = f32[12,7,7,9,512]{4,3,2,1,0:T(8,128)} reshape(f32[588,4608]{1,0:T(8,128)} %fusion.20) | data formatting | bytes 21676032 | tf_op jit(solution)/shard_map/reshape | solution.py:79
  649.9 32.4 %fusion.17 = (f32[12,7,7,1,512]{4,3,2,1,0:T(1,128)}, f32[12,7,7,1,512]{4,3,2,1,0:T(1,128)}, f32[12,7,7,1,512]{4,3,2,1,0:T(1,128)}, f32[12,7,7,1,512]{4,3,2,1,0:T...) fusion(f32[12,7,7,9,512]{4,3,2,1,0:T(8,128)} %reshape.498), kind=kLoop, calls=%fused_computation.119 | loop fusion | bytes 21676032 | tf_op jit(solution)/shard_map/slice | solution.py:85
  686.6 6.6 scatter-add.31
  697.9 6.5 scatter-add.34
  757.8 19.3 %all-reduce.8 = (f32[512]{0:T(512)S(1)}, f32[512]{0:T(512)S(1)}) all-reduce(f32[512]{0:T(512)S(1)} %get-tuple-element.143, f32[512]{0:T(512)S(1)} %get-tuple-element.142), channel_id=1, replica_groups=mesh['gx'=4,'gy'=8] {'gy'}, use_global_device_ids=true, to_apply=%region_38.39 | all-reduce | flops 1024 | bytes 8192 | tf_op jit(solution)/shard_map/psum | solution.py:8
  791.2 9.1 fusion.21
  801.1 31.7 %reduce-scatter.11.cloned.1.call-done = f32[512,512]{0,1:T(8,128)} async-done(((f32[2048,512]{0,1:T(8,128)}), f32[512,512]{0,1:T(8,128)}) %reduce-scatter.11.cloned.1.call-update) | async-done | bytes 1048592 | tf_op jit(solution)/shard_map/reduce_scatter | solution.py:207
  832.8 81.0 %reduce-scatter.15.cloned.1.call-done = f32[1152,512]{1,0:T(8,128)} async-done(((f32[4608,512]{1,0:T(8,128)}), f32[1152,512]{1,0:T(8,128)}) %reduce-scatter.15.cloned.1.call-update) | async-done | bytes 2359312 | tf_op jit(solution)/shard_map/reduce_scatter | solution.py:208
  917.6 39.9 %psum.153 = f32[]{:T(128)} all-reduce(f32[]{:T(128)} %get-tuple-element.217), channel_id=1, replica_groups=mesh['gx'=4,'gy'=8] {'gx','gy'}, use_global_device_ids=true, to_apply=%region_17.18 | all-reduce | flops 1 | bytes 8 | tf_op jit(solution)/shard_map/psum | solution.py:167
  958.1 6.6 convolution_add_fusion
  970.3 11.6 %reduce-scatter.19.cloned.1.call-done = f32[128,256]{1,0:T(8,128)} async-done(((f32[128,2048]{1,0:T(8,128)}), f32[128,256]{1,0:T(8,128)}) %reduce-scatter.19.cloned.1.call-update) | async-done | bytes 131088 | tf_op jit(solution)/shard_map/reduce_scatter | solution.py:214
  981.8 66.6 %reduce-scatter.13.cloned.1.call-done = f32[512,64]{0,1:T(8,128)} async-done(((f32[512,512]{0,1:T(8,128)}), f32[512,64]{0,1:T(8,128)}) %reduce-scatter.13.cloned.1.call-update) | async-done | bytes 131088 | tf_op jit(solution)/shard_map/reduce_scatter | solution.py:212
  1048.4 72.2 %reduce-scatter.21.cloned.1.call-done = f32[64,1152]{1,0:T(8,128)} async-done(((f32[512,1152]{1,0:T(8,128)}), f32[64,1152]{1,0:T(8,128)}) %reduce-scatter.21.cloned.1.call-update) | async-done | bytes 294928
  (216 shorter events, 215.6 us)
Async XLA Ops:
  7.2 47.7 %copy-start.19 = (bf16[128,256]{1,0:T(8,128)(2,1)S(1)}, bf16[128,256]{1,0:T(8,128)(2,1)}, u32[]{:S(2)}) copy-start(bf16[128,256]{1,0:T(8,128)(2,1)} %param.30) | copy-start | bytes 196612
  7.2 47.6 %all-gather.10.cloned.1.call-start = ((), (), s32[]{:S(2)}) async-start(), calls=%async_computation.7 | async-start | bytes 1327104 | tf_op jit(solution)/shard_map/all_gather | solution.py:15
  7.9 110.8 %all-gather.8.cloned.1.call-start = ((), (), s32[]{:S(2)}) async-start(), calls=%async_computation.6 | async-start | bytes 2621440 | tf_op jit(solution)/shard_map/all_gather | solution.py:20
  43.5 46.1 %copy-start.35 = (u32[32]{0:T(128)S(1)}, u32[32]{0:T(128)}, u32[]{:S(2)}) copy-start(u32[32]{0:T(128)} %constant.326) | copy-start | bytes 388
  43.5 47.4 %copy-start.34 = (bf16[192]{0:T(256)(128)(2,1)S(1)}, bf16[192]{0:T(256)(128)(2,1)}, u32[]{:S(2)}) copy-start(bf16[192]{0:T(256)(128)(2,1)} %param.31) | copy-start | bytes 1156
  43.6 152.4 %all-gather.12.cloned.1.call-start = ((), (), s32[]{:S(2)}) async-start(), calls=%async_computation.8 | async-start | bytes 5898240 | tf_op jit(solution)/shard_map/all_gather | solution.py:21
  54.8 192.2 %all-gather.14.cloned.1.call-start = ((), (), s32[]{:S(2)}) async-start(), calls=%async_computation.9 | async-start | bytes 2621440 | tf_op jit(solution)/shard_map/all_gather | solution.py:22
  88.2 277.0 %all-gather.16.cloned.1.call-start = ((), (), s32[]{:S(2)}) async-start(), calls=%async_computation.15 | async-start | bytes 2162688 | tf_op jit(solution)/shard_map/all_gather | solution.py:151
  118.6 410.0 %copy-start = (bf16[588,2048]{1,0:T(8,128)(2,1)}, bf16[588,2048]{1,0:T(8,128)(2,1)S(1)}, u32[]{:S(2)}) copy-start(bf16[588,2048]{1,0:T(8,128)(2,1)S(1)} %reshape.493) | copy-start | bytes 7225348
  162.1 28.9 %copy-start.20 = (f32[512]{0:T(512)}, f32[512]{0:T(512)S(1)}, u32[]{:S(2)}) copy-start(f32[512]{0:T(512)S(1)} %get-tuple-element.203) | copy-start | bytes 6148
  308.2 492.1 %reduce-scatter.17.cloned.1.call-start = ((), (), s32[]{:S(2)}) async-start(), calls=%async_computation.13 | async-start | bytes 5242880 | tf_op jit(solution)/shard_map/reduce_scatter | solution.py:209
  473.2 20.3 %collective-permute-start.6 = (f32[16,2048]{1,0:T(8,128)S(1)}, f32[16,2048]{1,0:T(8,128)S(1)}, u32[]{:S(2)}, u32[]{:S(2)}) collective-permute-start(f32[16,2048]{1,0:T(8,128)S(1)} %fusion), channel_id=1, source_target_pairs={{0,7},{1,8},{2,9},{3,10},{4,11},{5,12},{6,13},{7,14},{8,15},{9,16}... | collective-permute-start | bytes 393224
  480.3 16.8 %collective-permute-start.5 = (f32[16,2048]{1,0:T(8,128)S(1)}, f32[16,2048]{1,0:T(8,128)}, u32[]{:S(2)}, u32[]{:S(2)}) collective-permute-start(f32[16,2048]{1,0:T(8,128)S(1)} %fusion), channel_id=1, source_target_pairs={{0,6},{1,7},{2,8},{3,9},{4,10},{5,11},{6,12},{7,13},{8,14},{9,15},... | collective-permute-start | bytes 393224
  483.5 8.7 collective-permute-start.7
  486.2 15.7 %collective-permute-start.4 = (f32[16,2048]{1,0:T(8,128)S(1)}, f32[16,2048]{1,0:T(8,128)S(1)}, u32[]{:S(2)}, u32[]{:S(2)}) collective-permute-start(f32[16,2048]{1,0:T(8,128)S(1)} %fusion), channel_id=1, source_target_pairs={{0,5},{1,6},{2,7},{3,8},{4,9},{5,10},{6,11},{7,12},{8,13},{9,14},{... | collective-permute-start | bytes 393224
  488.1 13.8 %collective-permute-start.3 = (f32[16,2048]{1,0:T(8,128)S(1)}, f32[16,2048]{1,0:T(8,128)S(1)}, u32[]{:S(2)}, u32[]{:S(2)}) collective-permute-start(f32[16,2048]{1,0:T(8,128)S(1)} %fusion), channel_id=1, source_target_pairs={{0,4},{1,5},{2,6},{3,7},{4,8},{5,9},{6,10},{7,11},{8,12},{9,13},{1... | collective-permute-start | bytes 393224
  492.2 9.7 collective-permute-start.2
  493.5 8.4 collective-permute-start.1
  497.1 6.8 collective-permute-start
  585.1 6.2 copy-start.22
  585.1 6.2 copy-start.24
  585.7 5.5 copy-start.14
  595.2 237.6 %reduce-scatter.11.cloned.1.call-start = ((), (), s32[]{:S(2)}) async-start(), calls=%async_computation.10 | async-start | bytes 5242880 | tf_op jit(solution)/shard_map/reduce_scatter | solution.py:207
  756.0 26.7 %copy-start.33 = (f32[6144]{0:T(1024)S(1)}, f32[6144]{0:T(1024)}, u32[]{:S(2)}) copy-start(f32[6144]{0:T(1024)} %custom-call) | copy-start | bytes 73732
  756.0 28.1 %copy-start.30 = (f32[512]{0:T(512)S(1)}, f32[512]{0:T(512)}, u32[]{:S(2)}) copy-start(f32[512]{0:T(512)} %get-tuple-element.169) | copy-start | bytes 6148
  790.1 123.7 %reduce-scatter.15.cloned.1.call-start = ((), (), s32[]{:S(2)}) async-start(), calls=%async_computation.12 | async-start | bytes 11796480 | tf_op jit(solution)/shard_map/reduce_scatter | solution.py:208
  800.3 181.5 %reduce-scatter.19.cloned.1.call-start = ((), (), s32[]{:S(2)}) async-start(), calls=%async_computation.14 | async-start | bytes 1179648 | tf_op jit(solution)/shard_map/reduce_scatter | solution.py:214
  801.0 247.4 %reduce-scatter.13.cloned.1.call-start = ((), (), s32[]{:S(2)}) async-start(), calls=%async_computation.11 | async-start | bytes 1179648 | tf_op jit(solution)/shard_map/reduce_scatter | solution.py:212
  832.8 287.8 %reduce-scatter.21.cloned.1.call-start = ((), (), s32[]{:S(2)}) async-start(), calls=%async_computation.16 | async-start | bytes 2654208
  964.7 4.8 copy-start.27
  964.8 4.8 copy-start.25
  964.8 4.8 copy-start.23
  (23 other events, 48.5 us)
Sparse Core Ops, SparseCore 0:
  10.2 44.5 all-gather.9
  56.3 21.7 all-gather.7
  79.7 37.5 all-gather.11
  118.7 23.1 all-gather.13
  308.3 56.8 all-gather.15
  595.3 42.6 reduce-scatter.16
  790.2 42.4 reduce-scatter.10
  835.3 78.4 reduce-scatter.14
  917.8 64.0 reduce-scatter.18
  986.0 62.3 reduce-scatter.12
  1052.5 68.0 reduce-scatter.20
